TPU v7x, 32 devices: a whole 2x2x4 slice. The times are simulated.
32 devices in a mesh: groups: 2 (over x), ctx: 16 (over z, y, core).
Axes of the slice: x: 2, y: 2, z: 4, core: 2. Of those that a mesh axis runs over, the one named last changes fastest.
Arguments:
- queries: bfloat16 [128, 8192], P(('groups', 'ctx')), parts along dimension 0
- cache_keys: bfloat16 [49152, 512], P(('groups', 'ctx')), parts along dimension 0
- cached_value_rows: bfloat16 [49152, 512], P(('groups', 'ctx')), parts along dimension 0, may hold values from -5 to 5
- new_keys: bfloat16 [128, 512], P(('groups', 'ctx')), parts along dimension 0
- prompt_value_rows: bfloat16 [128, 512], P(('groups', 'ctx')), parts along dimension 0, may hold values from -5 to 5
- cache_len: int32 [32], P(('groups', 'ctx')), parts along dimension 0, may hold values from 1 to 1536, 15360 in all
- prompt_start: int32 [2], P('groups'), parts along dimension 0, may hold values from 7680 to 15360
Outputs:
- attended: bfloat16 [128, 8192], P(('groups', 'ctx')), parts along dimension 0
There are 2 independent parts, one for each index of `groups`. A program takes and returns all parts, laid end to end along the dimension named above; each array names one. Nothing has to cross between parts.
Inputs may be any that keep to these rules, and one draw needn't show every extreme that they name: cache_len sums to 15360; some shard is full.
All inputs are finite; a program needn't handle non-finite values.
Results may differ from a plain program's by a relative error of at most 0.0024.
Values may be sent and summed in bfloat16 or wider, within the bound.
No kernel may reach another device: no remote copies, remote signals or barrier semaphores. Data moves between devices by JAX's collectives and lax.ppermute only.
A program may use at most 64 MiB of HBM per device.

v0:
```python
import functools
import math

import jax
import jax.numpy as jnp
from jax import lax
from jax.experimental import pallas as pl
from jax.experimental.pallas import tpu as pltpu
from jax.sharding import PartitionSpec as P

KEY_VALUE_HEADS = 4
LANES = 128
CORES = 2
FLOOR = -1e30
TILE = 256
ATTEND_BYTES = 32 << 20
STAT_ROWS = 16
CHUNK_BLOCKS = 2
STEP = 2.0**15
MARGIN = 0.9998
F32 = jnp.float32
BF16 = jnp.bfloat16
I16 = jnp.int16
I32 = jnp.int32
VMEM = pl.BlockSpec(memory_space=pltpu.VMEM)
SMEM = pl.BlockSpec(memory_space=pltpu.SMEM)
SMALL = pltpu.CompilerParams(vmem_limit_bytes=8 << 20)


def encode(out, at, values, top, total):
    dims, width = values.shape
    largest = jnp.max(jnp.abs(values), axis=0, keepdims=True)
    exponent = jnp.floor(jnp.log2(jnp.maximum(largest, 1e-30))) + 1.0
    fixed = jnp.floor(values * (jnp.exp2(15.0 - exponent) * MARGIN) + 0.5)
    size = jnp.abs(top)
    level = jnp.zeros_like(top)
    scaled = top
    for i in range(1, 9):
        above = size >= STEP**i
        level = level + jnp.where(above, 1.0, 0.0)
        scaled = scaled * jnp.where(above, 1.0 / STEP, 1.0)
    a = jnp.floor(scaled)
    rest = (scaled - a) * STEP
    b = jnp.floor(rest)
    c = jnp.floor((rest - b) * STEP)
    logs = jnp.log2(total) * 1024.0
    la = jnp.floor(logs)
    lb = jnp.floor((logs - la) * STEP)
    row = lax.broadcasted_iota(I32, (STAT_ROWS, width), 0)
    stats = jnp.zeros((STAT_ROWS, width), F32)
    for i, part in enumerate((level, a, b, c, exponent, la, lb)):
        stats = jnp.where(row == i, part, stats)
    if not isinstance(at, int):
        at = pl.multiple_of(at, LANES)
    out[:dims, pl.ds(at, width)] = fixed.astype(I32).astype(I16)
    out[dims:, pl.ds(at, width)] = stats.astype(I32).astype(I16)


def decode_stats(ref, dims, at):
    stats = ref[dims:, at].astype(I32).astype(F32)

    def part(i):
        return stats[i : i + 1, :]

    top = part(1) + (part(2) + part(3) * (1.0 / STEP)) * (1.0 / STEP)
    for i in range(1, 9):
        top = top * jnp.where(part(0) >= i, STEP, 1.0)
    total = jnp.exp2((part(5) + part(6) * (1.0 / STEP)) * (1.0 / 1024.0))
    return top, total, jnp.exp2(part(4) - 15.0) * (1.0 / MARGIN)


def join_kernel(length, length_other, mine, queries_other, out):
    rows, half = mine.shape
    core = lax.axis_index("ctx") % CORES
    other = queries_other[:, pl.ds(pl.multiple_of(core * half, LANES), half)]
    out[:, :half] = jnp.concatenate([mine[...].astype(F32), other.astype(F32)], axis=0).astype(BF16)
    lane = lax.broadcasted_iota(I32, (CORES * rows, LANES), 1)
    row = lax.broadcasted_iota(I32, (CORES * rows, LANES), 0)
    count = jnp.where(row < rows, length[0], length_other[0])
    coded = jnp.where(lane == 0, count // LANES, jnp.where(lane == 1, count % LANES, 0))
    out[:, half:] = coded.astype(F32).astype(BF16)


def join(length, length_other, mine, queries_other):
    rows, half = mine.shape
    return pl.pallas_call(
        join_kernel,
        out_shape=jax.ShapeDtypeStruct((CORES * rows, half + LANES), BF16),
        in_specs=[SMEM, SMEM, VMEM, VMEM],
        out_specs=VMEM,
        compiler_params=SMALL,
    )(length, length_other, mine, queries_other)


def attend_kernel(sizes, *refs):
    own_rows, orders, group, kv_heads, sets, first, chosen = sizes
    start = refs[0]
    gathered = refs[1 : 1 + sets]
    fresh_a, fresh_b, keys_a, keys_b, values_a, values_b = refs[1 + sets : 7 + sets]
    out, query_t, scores, sums, tops, totals = refs[7 + sets :]
    queries = gathered[first : first + chosen]
    chip_rows = CORES * own_rows
    slots = keys_a.shape[0]
    count = gathered[0].shape[0]
    tokens = min(count, CHUNK_BLOCKS * chip_rows)
    blocks = tokens // chip_rows
    set_blocks = count // chip_rows
    set_lanes = tokens * group
    lanes = chosen * set_lanes
    me = lax.axis_index("ctx")
    core, chip = me % CORES, me // CORES
    factor = math.log2(math.e) / math.sqrt(LANES)
    heads = range(kv_heads)

    steps = [jnp.where(core == 0, a // CORES, b // CORES) for a, b in zip(*orders)]

    def origin(block):
        off = jnp.zeros_like(block)
        for i, step in enumerate(steps):
            off = off ^ jnp.where((block >> i) & 1 == 1, step, 0)
        return chip ^ off

    found = [0.0, 0.0, 0.0]
    for i, ref in enumerate(gathered):
        rows = ref.shape[0]
        lane = lax.broadcasted_iota(I32, (rows, LANES), 1)
        row = lax.broadcasted_iota(I32, (rows, LANES), 0)
        place = origin(row // chip_rows + i * set_blocks)
        inside = row % chip_rows
        counts = jnp.where(lane == 0, float(LANES), 1.0) * ref[:, ref.shape[1] - LANES :].astype(F32)
        counts = jnp.where((inside % own_rows == 0) & (lane < 2), counts, 0.0)
        here = place == chip
        second = inside >= own_rows
        for k, wanted in enumerate((place < chip, here & ~second, here & second)):
            found[k] = found[k] + jnp.sum(jnp.where(wanted, counts, 0.0), axis=0, keepdims=True)
    row = lax.broadcasted_iota(I32, (8, LANES), 0)
    found = functools.reduce(lambda x, k: jnp.where(row == k, found[k], x), range(3), jnp.zeros((8, LANES), F32))
    found = jnp.sum(found, axis=1, keepdims=True).astype(I32)
    before, length = found[0, 0], [found[1, 0], found[2, 0]]
    begins = [
        before + jnp.where(core == 1, length[1], 0),
        before + jnp.where(core == 0, length[0], 0),
    ]
    limits = [jnp.clip(jnp.minimum(n, start[0] - at), 0, slots) for n, at in zip(length, begins)]

    def attend_chunk(chunk, carry):
        key_row = lax.broadcasted_iota(I32, (chip_rows, lanes), 0)
        lane = lax.broadcasted_iota(I32, (chip_rows, lanes), 1)
        part = key_row // own_rows
        key_id = (chip * CORES + (core ^ part)) * own_rows + key_row % own_rows
        inside = lane % chip_rows
        block = (lane // set_lanes + first) * set_blocks + lane % set_lanes // (group * chip_rows) + chunk * blocks
        token = (origin(block) * CORES + (core ^ (inside // own_rows))) * own_rows + inside % own_rows
        causal = key_id <= token
        nothing = jnp.zeros((16 - chip_rows % 16, LANES), F32)
        fresh_scores, fresh_values = [], []

        for h in heads:
            rows = pl.ds(pl.multiple_of(chunk * tokens, tokens), tokens)
            q = jnp.concatenate(
                [
                    ref[rows, (h * group + g) * LANES : (h * group + g + 1) * LANES].astype(F32)[b * chip_rows :][:chip_rows]
                    for ref in queries
                    for b in range(blocks)
                    for g in range(group)
                ],
                axis=0,
            )
            query_t[h] = q.T.astype(BF16)
            at = pl.multiple_of((core * kv_heads + h) * LANES, LANES)

            mine = fresh_a[:, pl.ds(at, LANES)].astype(F32)
            theirs = fresh_b[:, pl.ds(at, LANES)].astype(F32)
            new_keys = jnp.concatenate([mine[:own_rows], theirs[:own_rows], nothing], 0).astype(BF16)
            new_values = jnp.concatenate([mine[own_rows:], theirs[own_rows:], nothing], 0).astype(BF16)
            fresh_values.append(new_values)
            fresh_scores.append(jnp.dot(new_keys, query_t[h], preferred_element_type=F32)[:chip_rows] * factor)

        def fold(tile, combine):
            return combine(tile.reshape(tile.shape[0] // 8, 8, lanes), axis=0)

        tn = (((0,), (0,)), ((), ()))

        def shard(s, keys, values, tiles):
            seen = causal & (part == s)
            filled = limits[s] - (tiles - 1) * TILE

            def columns(h):
                return pl.ds(pl.multiple_of((core * kv_heads * LANES if s else 0) + h * LANES, LANES), LANES)

            pieces = [slice(0, (tiles - 1) * TILE)] * (tiles > 1) + [slice((tiles - 1) * TILE, tiles * TILE)] * (tiles > 0)
            top = []
            for h in heads:
                peak = jnp.where(seen, fresh_scores[h], FLOOR)
                for rows in pieces:
                    tile = jnp.dot(keys[rows, columns(h)], query_t[h], preferred_element_type=F32) * factor
                    if rows is pieces[-1]:
                        tile = jnp.where(lax.broadcasted_iota(I32, tile.shape, 0) < filled, tile, FLOOR)
                    scores[h, rows, :] = tile
                    peak = jnp.maximum(peak, fold(tile, jnp.max))
                top.append(jnp.max(peak, axis=0, keepdims=True))
            for h in heads:
                weight = jnp.where(seen, jnp.exp2(fresh_scores[h] - top[h]), 0.0)
                padded = jnp.concatenate([weight, jnp.zeros((16 - chip_rows % 16, lanes), F32)], 0).astype(BF16)
                summed = lax.dot_general(fresh_values[h], padded, tn, preferred_element_type=F32)
                mass = weight
                for rows in pieces:
                    weight = jnp.exp2(scores[h, rows, :] - top[h])
                    if rows is pieces[-1]:
                        weight = jnp.where(lax.broadcasted_iota(I32, weight.shape, 0) < filled, weight, 0.0)
                    summed = summed + lax.dot_general(
                        values[rows, columns(h)], weight.astype(BF16), tn, preferred_element_type=F32
                    )
                    mass = mass + fold(weight, jnp.sum)
                sums[s, h] = summed
                tops[s, h] = top[h]
                totals[s, h] = jnp.sum(mass, axis=0, keepdims=True)

        for s, (keys, values) in enumerate(((keys_a, values_a), (keys_b, values_b))):
            needed = (limits[s] + TILE - 1) // TILE
            for tiles in range(slots // TILE + 1):
                pl.when(needed == tiles)(functools.partial(shard, s, keys, values, tiles))

        for h in heads:
            top_a, top_b = tops[0, h], tops[1, h]
            top = jnp.maximum(top_a, top_b)
            scale_a = jnp.exp2(top_a - top)
            scale_b = jnp.exp2(top_b - top)
            total = jnp.maximum(totals[0, h] * scale_a + totals[1, h] * scale_b, 1.0)
            merged = sums[0, h] * (scale_a / total) + sums[1, h] * (scale_b / total)
            width = group * chip_rows
            for i in range(chosen):
                for b in range(blocks):
                    at = i * set_lanes + b * width
                    cut = slice(at, at + width)
                    place = ((i * set_blocks + chunk * blocks + b) * kv_heads + h) * width
                    encode(out, place, merged[:, cut], top[:, cut], total[:, cut])
        return carry

    chunks = count // tokens
    if chunks == 1:
        attend_chunk(0, 0)
    else:
        lax.fori_loop(0, chunks, attend_chunk, 0)


def attend(start, gathered, chosen, fresh, cache, *, own_rows, orders):
    first, end = chosen
    count = gathered[0].shape[0]
    chip_rows = CORES * own_rows
    tokens = min(count, CHUNK_BLOCKS * chip_rows)
    slots = cache[0].shape[0]
    kv_heads = cache[0].shape[1] // LANES
    heads = gathered[0].shape[1] // LANES - 1
    group = heads // kv_heads
    lanes = (end - first) * tokens * group
    sizes = (own_rows, orders, group, kv_heads, len(gathered), first, end - first)
    return pl.pallas_call(
        functools.partial(attend_kernel, sizes),
        out_shape=jax.ShapeDtypeStruct((LANES + STAT_ROWS, (end - first) * count * heads), I16),
        in_specs=[SMEM] + [VMEM] * (len(gathered) + 6),
        out_specs=VMEM,
        scratch_shapes=[
            pltpu.VMEM((kv_heads, LANES, lanes), BF16),
            pltpu.VMEM((kv_heads, slots, lanes), F32),
            pltpu.VMEM((2, kv_heads, LANES, lanes), F32),
            pltpu.VMEM((2, kv_heads, 1, lanes), F32),
            pltpu.VMEM((2, kv_heads, 1, lanes), F32),
        ],
        compiler_params=pltpu.CompilerParams(vmem_limit_bytes=ATTEND_BYTES),
    )(start, *gathered, *fresh, *cache)


def merged_part(refs, dims, at):
    stats = [decode_stats(ref, dims, at) for ref in refs]
    top = functools.reduce(jnp.maximum, [x[0] for x in stats])
    masses = [x[1] * jnp.exp2(x[0] - top) for x in stats]
    total = functools.reduce(jnp.add, masses)
    values = 0.0
    for ref, mass, (_, _, unit) in zip(refs, masses, stats):
        values = values + ref[:dims, at].astype(I32).astype(F32) * (mass / total * unit)
    return values, top, total


def merge_kernel(inputs, *refs):
    parts, outs = refs[:inputs], refs[inputs:]
    dims = parts[0].shape[0] - STAT_ROWS
    width = outs[0].shape[1]
    step = min(width, 2 * LANES)
    for i, out in reversed(list(enumerate(outs))):
        for at in range(0, width, step):
            encode(out, at, *merged_part(parts, dims, slice(i * width + at, i * width + at + step)))


def merge(parts, pieces):
    rows, width = parts[0].shape
    shape = jax.ShapeDtypeStruct((rows, width // pieces), I16)
    return pl.pallas_call(
        functools.partial(merge_kernel, len(parts)),
        out_shape=(shape,) * pieces,
        in_specs=[VMEM] * len(parts),
        out_specs=(VMEM,) * pieces,
        compiler_params=SMALL,
    )(*parts)


def finish_kernel(group, inputs, *refs):
    parts, (mine, other) = refs[:inputs], refs[inputs:]
    dims = parts[0].shape[0] - STAT_ROWS
    own_rows = mine.shape[0]
    chip_rows = CORES * own_rows
    width = group * chip_rows
    for h in range(parts[0].shape[1] // width):
        values, _, _ = merged_part(parts, dims, slice(h * width, (h + 1) * width))
        rows = values.T
        for g in range(group):
            at = (h * group + g) * dims
            tokens = rows[g * chip_rows : (g + 1) * chip_rows]
            mine[:, at : at + dims] = tokens[:own_rows].astype(BF16)
            other[:, at : at + dims] = tokens[own_rows:].astype(BF16)


def finish(parts, own_rows, group):
    rows, width = parts[0].shape
    shape = jax.ShapeDtypeStruct((own_rows, width // (CORES * own_rows) * (rows - STAT_ROWS)), BF16)
    return pl.pallas_call(
        functools.partial(finish_kernel, group, len(parts)),
        out_shape=(shape, shape),
        in_specs=[VMEM] * len(parts),
        out_specs=(VMEM, VMEM),
        compiler_params=SMALL,
    )(*parts)


def place_kernel(mine, theirs, out):
    half = mine.shape[1]
    core = lax.axis_index("ctx") % CORES
    out[:, pl.ds(pl.multiple_of(core * half, LANES), half)] = mine[...]
    out[:, pl.ds(pl.multiple_of((1 - core) * half, LANES), half)] = theirs[...]


def place(mine, theirs):
    rows, half = mine.shape
    return pl.pallas_call(
        place_kernel,
        out_shape=jax.ShapeDtypeStruct((rows, CORES * half), BF16),
        in_specs=[VMEM, VMEM],
        out_specs=VMEM,
        compiler_params=SMALL,
    )(mine, theirs)


def per_device(
    queries, cache_keys, cached_value_rows, new_keys, prompt_value_rows, cache_len, prompt_start
):
    width = lax.axis_size("ctx")
    own_rows = queries.shape[0]
    group = queries.shape[1] // cache_keys.shape[1]
    bits = [CORES << i for i in range((width // CORES).bit_length() - 1)]
    orders = (tuple(bits[-1:] + bits[:-1]), tuple(bits[-2:] + bits[:-2]))
    odd = len(bits) % 2
    stages = [(0,)] * odd + [(i, i + 1) for i in range(odd, len(bits), 2)]

    def swap(x):
        return lax.ppermute(x, "ctx", [(i, i ^ 1) for i in range(width)])

    def partners(stage):
        return [
            [sum(order[bit] for k, bit in enumerate(stage) if c >> k & 1) for order in orders]
            for c in range(1, 1 << len(stage))
        ]

    def exchange(x, distance):
        return lax.ppermute(x, "ctx", [(i, i ^ distance[i % CORES]) for i in range(width)])

    def own_half(x):
        half = x.shape[1] // CORES
        return lax.dynamic_slice_in_dim(x, core * half, half, 1)

    core = lax.axis_index("ctx") % CORES
    held = join(cache_len, swap(cache_len), own_half(queries), swap(queries))
    cache_keys, cached_value_rows, held = lax.optimization_barrier((cache_keys, cached_value_rows, held))
    cache = [y for x in (cache_keys, cached_value_rows) for y in (own_half(x), swap(x))]
    for stage in stages:
        gathered = [held] + [exchange(held, distance) for distance in partners(stage)]
        if stage != stages[-1]:
            held = jnp.concatenate(gathered, axis=0)
    cache[0], cache[2], prompt_start = lax.optimization_barrier((cache[0], cache[2], prompt_start))
    gathered[-1], cache[0], cache[2], new_keys, prompt_value_rows = lax.optimization_barrier(
        (gathered[-1], cache[0], cache[2], new_keys, prompt_value_rows)
    )
    fresh = jnp.concatenate([new_keys, prompt_value_rows], axis=0)
    fresh = [fresh, swap(fresh)]
    half = len(gathered) // 2
    far, near = (
        attend(prompt_start, gathered, chosen, fresh, cache, own_rows=own_rows, orders=orders)
        for chosen in ((half, 2 * half), (0, half))
    )
    last = len(bits) - 1
    parts = [near, exchange(far, partners((last,))[0])]
    for stage in [(i - 1, i) if i else (i,) for i in range(last - 1, -1, -2)]:
        parts = merge(parts, 1 << len(stage))
        parts = [parts[0]] + [exchange(x, distance) for x, distance in zip(parts[1:], partners(stage))]
    mine, other = finish(parts, own_rows, group)
    return place(mine, swap(other))


def solution(mesh):
    return jax.shard_map(
        per_device,
        mesh=mesh,
        in_specs=(
            P(("groups", "ctx"), None),
            P(("groups", "ctx"), None),
            P(("groups", "ctx"), None),
            P(("groups", "ctx"), None),
            P(("groups", "ctx"), None),
            P(("groups", "ctx")),
            P("groups"),
        ),
        out_specs=P(("groups", "ctx"), None),
        check_vma=False,
    )
```

profile of v0, /device:TPU:0, one launch (start us, length us, event | category | flops | bytes accessed | tf_op | source)
XLA Modules:
  0.0 43.4 jit_solution(2066880825238627665)
XLA Ops:
  0.0 0.5 %collective-permute-start = (s32[1]{0:T(128)}, s32[1]{0:T(128)}, u32[]{:S(2)}, u32[]{:S(2)}) collective-permute-start(s32[1]{0:T(128)} %param.12), channel_id=1, source_target_pairs={{0,1},{1,0},{2,3},{3,2},{4,5},{5,4},{6,7},{7,6},{8,9},{9,8},{10,11... | collective-permute-start | bytes 20 | tf_op jit(solution)/shard_map/ppermute | solution.py:365
  0.5 0.1 collective-permute-start.1
  0.5 0.8 %constant_dynamic-slice_fusion.2.mine = bf16[4,4096]{1,0:T(4,128)(2,1)S(1)} fusion(bf16[4,8192]{1,0:T(4,128)(2,1)} %param.7, s32[]{:T(128)S(6)} %select_n.15), kind=kLoop, calls=%fused_computation.5 | loop fusion | bytes 65540 | tf_op jit(solution)/shard_map/dynamic_slice | solution.py:378
  1.9 0.0 collective-permute-done.length_other
  1.9 0.0 collective-permute-done.1.queries_other
  2.0 0.7 %shard_map.73 = bf16[8,4224]{1,0:T(8,128)(2,1)S(1)} custom-call(s32[1]{0:T(128)S(6)} %copy.9.length, s32[1]{0:T(128)} %collective-permute-done.length_other, bf16[4,4096]{1,0:T(4,128)(2,1)S(1)} %constant_dynamic-slice_fusion.2.mine, bf16[4,8192]{1,0:T(4,128)(2,1)S(1)} %collective-permute-done.1.queries_other), custom_call_target="tpu_custom_call" | custom-call | tf_op jit(solution)/shard_map/pallas_call | solution.py:86
  2.7 0.5 %collective-permute-start.7 = (bf16[1536,512]{1,0:T(8,128)(2,1)}, bf16[1536,512]{1,0:T(8,128)(2,1)S(1)}, u32[]{:S(2)}, u32[]{:S(2)}) collective-permute-start(bf16[1536,512]{1,0:T(8,128)(2,1)} %param.8), channel_id=1, source_target_pairs={{0,1},{1,0},{2,3},{3,2},{4,5},{5,4},{6,7},{7,6},{8,9},{9,8},{10,11... | collective-permute-start | bytes 4718600 | tf_op jit(solution)/shard_map/ppermute | solution.py:365
  3.2 0.1 collective-permute-start.8
  3.3 4.0 %collective-permute-start.2 = (bf16[8,4224]{1,0:T(8,128)(2,1)S(1)}, bf16[8,4224]{1,0:T(8,128)(2,1)S(1)}, u32[]{:S(2)}, u32[]{:S(2)}) collective-permute-start(bf16[8,4224]{1,0:T(8,128)(2,1)S(1)} %shard_map.73), channel_id=1, source_target_pairs={{0,8},{1,5},{2,10},{3,7},{4,12},{5,1},{6,14},{7,3},{8,0},{9,13},{1... | collective-permute-start | bytes 202760 | tf_op jit(solution)/shard_map/ppermute | solution.py:374
  7.3 2.3 %collective-permute-done.2 = bf16[8,4224]{1,0:T(8,128)(2,1)S(1)} collective-permute-done((bf16[8,4224]{1,0:T(8,128)(2,1)S(1)}, bf16[8,4224]{1,0:T(8,128)(2,1)S(1)}, u32[]{:S(2)}, u32[]{:S(2)}) %collective-permute-start.2) | collective-permute-done | bytes 67616 | tf_op jit(solution)/shard_map/ppermute | solution.py:374
  9.6 0.0 copy-start
  9.6 0.0 copy-start.1
  9.6 2.9 %collective-permute-start.5 = (bf16[16,4224]{1,0:T(8,128)(2,1)S(1)}, bf16[16,4224]{1,0:T(8,128)(2,1)S(1)}, u32[]{:S(2)}, u32[]{:S(2)}) collective-permute-start(bf16[16,4224]{1,0:T(8,128)(2,1)S(1)} %constant_dynamic-update-slice_fusion.refs_1_), channel_id=1, source_target_pairs={{0,6},{1,11},{2,4},{3,9},{4,2},{5,15},{6,0},{7,13},{8,14},{9,3},{1... | collective-permute-start | bytes 405512 | tf_op jit(solution)/shard_map/ppermute | solution.py:374
  12.5 0.4 %collective-permute-start.4 = (bf16[16,4224]{1,0:T(8,128)(2,1)S(1)}, bf16[16,4224]{1,0:T(8,128)(2,1)S(1)}, u32[]{:S(2)}, u32[]{:S(2)}) collective-permute-start(bf16[16,4224]{1,0:T(8,128)(2,1)S(1)} %constant_dynamic-update-slice_fusion.refs_1_), channel_id=1, source_target_pairs={{0,4},{1,3},{2,6},{3,1},{4,0},{5,7},{6,2},{7,5},{8,12},{9,11},{10,... | collective-permute-start | bytes 405512 | tf_op jit(solution)/shard_map/ppermute | solution.py:374
  13.0 0.2 collective-permute-start.3
  13.2 1.5 %constant_dynamic-slice_fusion = (bf16[1536,256]{1,0:T(8,128)(2,1)S(1)}, bf16[1536,256]{1,0:T(8,128)(2,1)S(1)}) fusion(bf16[1536,512]{1,0:T(8,128)(2,1)} %param.9, s32[]{:T(128)S(6)} %select_n.16, bf16[1536,512]{1,0:T(8,128)(2,1)} %param.8), kind=kLoop, calls=%fused_computation.3 | loop fusion | bytes 3145732 | tf_op jit(solution)/shard_map/dynamic_slice | solution.py:378
  14.6 1.4 %collective-permute-done.5.refs_4_ = bf16[16,4224]{1,0:T(8,128)(2,1)S(1)} collective-permute-done((bf16[16,4224]{1,0:T(8,128)(2,1)S(1)}, bf16[16,4224]{1,0:T(8,128)(2,1)S(1)}, u32[]{:S(2)}, u32[]{:S(2)}) %collective-permute-start.5) | collective-permute-done | bytes 135200 | tf_op jit(solution)/shard_map/ppermute | solution.py:374
  16.0 0.0 copy-done
  16.1 0.0 copy-done.1
  16.1 0.1 collective-permute-start.6
  16.8 2.4 %collective-permute-done.4.refs_3_ = bf16[16,4224]{1,0:T(8,128)(2,1)S(1)} collective-permute-done((bf16[16,4224]{1,0:T(8,128)(2,1)S(1)}, bf16[16,4224]{1,0:T(8,128)(2,1)S(1)}, u32[]{:S(2)}, u32[]{:S(2)}) %collective-permute-start.4) | collective-permute-done | bytes 135200 | tf_op jit(solution)/shard_map/ppermute | solution.py:374
  19.2 0.0 collective-permute-done.3.refs_2_
  19.2 0.0 collective-permute-done.6.refs_6_
  19.2 0.0 collective-permute-done.7.refs_8_
  19.2 0.0 collective-permute-done.8.refs_10_
  19.2 4.9 %shard_map.75 = s16[144,1024]{1,0:T(8,128)(2,1)S(1)} custom-call(s32[1]{0:T(128)S(6)} %copy.10.refs_0_, bf16[16,4224]{1,0:T(8,128)(2,1)S(1)} %constant_dynamic-update-slice_fusion.refs_1_, bf16[16,4224]{1,0:T(8,128)(2,1)S(1)} %collective-permute-done.3.refs_2_, bf16[16,4224]{1,0:T(8,128)(2,1)S(1)} %collective-permute-done.4.refs_3_, ...), custom_call_target="tpu_custom_call" | custom-call | tf_op jit(solution)/shard_map/pallas_call | solution.py:258
  24.1 0.1 collective-permute-start.9
  24.2 4.9 %shard_map.74.refs_0_ = s16[144,1024]{1,0:T(8,128)(2,1)S(1)} custom-call(s32[1]{0:T(128)S(6)} %copy.10.refs_0_, bf16[16,4224]{1,0:T(8,128)(2,1)S(1)} %constant_dynamic-update-slice_fusion.refs_1_, bf16[16,4224]{1,0:T(8,128)(2,1)S(1)} %collective-permute-done.3.refs_2_, bf16[16,4224]{1,0:T(8,128)(2,1)S(1)} %collective-permute-done.4.refs_3_, ...), custom_call_target="tpu_custom_call" | custom-call | tf_op jit(solution)/shard_map/pallas_call | solution.py:258
  29.1 1.8 %collective-permute-done.9.refs_1_ = s16[144,1024]{1,0:T(8,128)(2,1)S(1)} collective-permute-done((s16[144,1024]{1,0:T(8,128)(2,1)S(1)}, s16[144,1024]{1,0:T(8,128)(2,1)S(1)}, u32[]{:S(2)}, u32[]{:S(2)}) %collective-permute-start.9) | collective-permute-done | bytes 294944 | tf_op jit(solution)/shard_map/ppermute | solution.py:374
  30.9 0.4 shard_map.76
  31.3 2.2 %collective-permute-start.10 = (s16[144,256]{1,0:T(8,128)(2,1)S(1)}, s16[144,256]{1,0:T(8,128)(2,1)S(1)}, u32[]{:S(2)}, u32[]{:S(2)}) collective-permute-start(s16[144,256]{1,0:T(8,128)(2,1)S(1)} %get-tuple-element.34), channel_id=1, source_target_pairs={{0,8},{1,5},{2,10},{3,7},{4,12},{5,1},{6,14},{7,3},{8,0},{9,13},{1... | collective-permute-start | bytes 221192 | tf_op jit(solution)/shard_map/ppermute | solution.py:374
  33.5 0.2 collective-permute-start.11
  33.8 2.0 %collective-permute-start.12 = (s16[144,256]{1,0:T(8,128)(2,1)S(1)}, s16[144,256]{1,0:T(8,128)(2,1)S(1)}, u32[]{:S(2)}, u32[]{:S(2)}) collective-permute-start(s16[144,256]{1,0:T(8,128)(2,1)S(1)} %get-tuple-element.36), channel_id=1, source_target_pairs={{0,10},{1,13},{2,8},{3,15},{4,14},{5,9},{6,12},{7,11},{8,2},{9,5},... | collective-permute-start | bytes 221192 | tf_op jit(solution)/shard_map/ppermute | solution.py:374
  35.8 3.9 %collective-permute-done.10.refs_1_ = s16[144,256]{1,0:T(8,128)(2,1)S(1)} collective-permute-done((s16[144,256]{1,0:T(8,128)(2,1)S(1)}, s16[144,256]{1,0:T(8,128)(2,1)S(1)}, u32[]{:S(2)}, u32[]{:S(2)}) %collective-permute-start.10) | collective-permute-done | bytes 73760 | tf_op jit(solution)/shard_map/ppermute | solution.py:374
  39.7 0.0 collective-permute-done.11.refs_2_
  39.7 1.6 %collective-permute-done.12.refs_3_ = s16[144,256]{1,0:T(8,128)(2,1)S(1)} collective-permute-done((s16[144,256]{1,0:T(8,128)(2,1)S(1)}, s16[144,256]{1,0:T(8,128)(2,1)S(1)}, u32[]{:S(2)}, u32[]{:S(2)}) %collective-permute-start.12) | collective-permute-done | bytes 73760 | tf_op jit(solution)/shard_map/ppermute | solution.py:374
  41.3 0.2 shard_map.77
  41.5 0.1 collective-permute-start.13
  41.6 1.2 %collective-permute-done.13.theirs = bf16[4,4096]{1,0:T(4,128)(2,1)S(1)} collective-permute-done((bf16[4,4096]{1,0:T(4,128)(2,1)S(1)}, bf16[4,4096]{1,0:T(4,128)(2,1)S(1)}, u32[]{:S(2)}, u32[]{:S(2)}) %collective-permute-start.13) | collective-permute-done | bytes 32800 | tf_op jit(solution)/shard_map/ppermute | solution.py:365
  42.8 0.6 %shard_map.78 = bf16[4,8192]{1,0:T(4,128)(2,1)} custom-call(bf16[4,4096]{1,0:T(4,128)(2,1)S(1)} %get-tuple-element.37.mine, bf16[4,4096]{1,0:T(4,128)(2,1)S(1)} %collective-permute-done.13.theirs), custom_call_target="tpu_custom_call" | custom-call | tf_op jit(solution)/shard_map/pallas_call | solution.py:344
  (3 shorter events, 0.0 us)
Async XLA Ops:
  0.0 1.9 %collective-permute-start = (s32[1]{0:T(128)}, s32[1]{0:T(128)}, u32[]{:S(2)}, u32[]{:S(2)}) collective-permute-start(s32[1]{0:T(128)} %param.12), channel_id=1, source_target_pairs={{0,1},{1,0},{2,3},{3,2},{4,5},{5,4},{6,7},{7,6},{8,9},{9,8},{10,11... | collective-permute-start | bytes 20 | tf_op jit(solution)/shard_map/ppermute | solution.py:365
  0.5 1.5 %collective-permute-start.1 = (bf16[4,8192]{1,0:T(4,128)(2,1)}, bf16[4,8192]{1,0:T(4,128)(2,1)S(1)}, u32[]{:S(2)}, u32[]{:S(2)}) collective-permute-start(bf16[4,8192]{1,0:T(4,128)(2,1)} %param.7), channel_id=1, source_target_pairs={{0,1},{1,0},{2,3},{3,2},{4,5},{5,4},{6,7},{7,6},{8,9},{9,8},{10,11... | collective-permute-start | bytes 196616 | tf_op jit(solution)/shard_map/ppermute | solution.py:365
  2.7 16.5 %collective-permute-start.7 = (bf16[1536,512]{1,0:T(8,128)(2,1)}, bf16[1536,512]{1,0:T(8,128)(2,1)S(1)}, u32[]{:S(2)}, u32[]{:S(2)}) collective-permute-start(bf16[1536,512]{1,0:T(8,128)(2,1)} %param.8), channel_id=1, source_target_pairs={{0,1},{1,0},{2,3},{3,2},{4,5},{5,4},{6,7},{7,6},{8,9},{9,8},{10,11... | collective-permute-start | bytes 4718600 | tf_op jit(solution)/shard_map/ppermute | solution.py:365
  3.2 16.0 %collective-permute-start.8 = (bf16[1536,512]{1,0:T(8,128)(2,1)}, bf16[1536,512]{1,0:T(8,128)(2,1)S(1)}, u32[]{:S(2)}, u32[]{:S(2)}) collective-permute-start(bf16[1536,512]{1,0:T(8,128)(2,1)} %param.9), channel_id=1, source_target_pairs={{0,1},{1,0},{2,3},{3,2},{4,5},{5,4},{6,7},{7,6},{8,9},{9,8},{10,11... | collective-permute-start | bytes 4718600 | tf_op jit(solution)/shard_map/ppermute | solution.py:365
  3.3 6.3 %collective-permute-start.2 = (bf16[8,4224]{1,0:T(8,128)(2,1)S(1)}, bf16[8,4224]{1,0:T(8,128)(2,1)S(1)}, u32[]{:S(2)}, u32[]{:S(2)}) collective-permute-start(bf16[8,4224]{1,0:T(8,128)(2,1)S(1)} %shard_map.73), channel_id=1, source_target_pairs={{0,8},{1,5},{2,10},{3,7},{4,12},{5,1},{6,14},{7,3},{8,0},{9,13},{1... | collective-permute-start | bytes 202760 | tf_op jit(solution)/shard_map/ppermute | solution.py:374
  9.6 6.5 %copy-start = (bf16[4,512]{1,0:T(4,128)(2,1)S(1)}, bf16[4,512]{1,0:T(4,128)(2,1)}, u32[]{:S(2)}) copy-start(bf16[4,512]{1,0:T(4,128)(2,1)} %param.11) | copy-start | bytes 12292
  9.6 6.5 %copy-start.1 = (bf16[4,512]{1,0:T(4,128)(2,1)S(1)}, bf16[4,512]{1,0:T(4,128)(2,1)}, u32[]{:S(2)}) copy-start(bf16[4,512]{1,0:T(4,128)(2,1)} %param.10) | copy-start | bytes 12292
  9.6 6.5 %collective-permute-start.5 = (bf16[16,4224]{1,0:T(8,128)(2,1)S(1)}, bf16[16,4224]{1,0:T(8,128)(2,1)S(1)}, u32[]{:S(2)}, u32[]{:S(2)}) collective-permute-start(bf16[16,4224]{1,0:T(8,128)(2,1)S(1)} %constant_dynamic-update-slice_fusion.refs_1_), channel_id=1, source_target_pairs={{0,6},{1,11},{2,4},{3,9},{4,2},{5,15},{6,0},{7,13},{8,14},{9,3},{1... | collective-permute-start | bytes 405512 | tf_op jit(solution)/shard_map/ppermute | solution.py:374
  12.5 6.7 %collective-permute-start.4 = (bf16[16,4224]{1,0:T(8,128)(2,1)S(1)}, bf16[16,4224]{1,0:T(8,128)(2,1)S(1)}, u32[]{:S(2)}, u32[]{:S(2)}) collective-permute-start(bf16[16,4224]{1,0:T(8,128)(2,1)S(1)} %constant_dynamic-update-slice_fusion.refs_1_), channel_id=1, source_target_pairs={{0,4},{1,3},{2,6},{3,1},{4,0},{5,7},{6,2},{7,5},{8,12},{9,11},{10,... | collective-permute-start | bytes 405512 | tf_op jit(solution)/shard_map/ppermute | solution.py:374
  13.0 6.2 %collective-permute-start.3 = (bf16[16,4224]{1,0:T(8,128)(2,1)S(1)}, bf16[16,4224]{1,0:T(8,128)(2,1)S(1)}, u32[]{:S(2)}, u32[]{:S(2)}) collective-permute-start(bf16[16,4224]{1,0:T(8,128)(2,1)S(1)} %constant_dynamic-update-slice_fusion.refs_1_), channel_id=1, source_target_pairs={{0,2},{1,9},{2,0},{3,11},{4,6},{5,13},{6,4},{7,15},{8,10},{9,1},{1... | collective-permute-start | bytes 405512 | tf_op jit(solution)/shard_map/ppermute | solution.py:374
  16.1 3.1 %collective-permute-start.6 = (bf16[8,512]{1,0:T(8,128)(2,1)S(1)}, bf16[8,512]{1,0:T(8,128)(2,1)S(1)}, u32[]{:S(2)}, u32[]{:S(2)}) collective-permute-start(bf16[8,512]{1,0:T(8,128)(2,1)S(1)} %pad_maximum_fusion.refs_5_), channel_id=1, source_target_pairs={{0,1},{1,0},{2,3},{3,2},{4,5},{5,4},{6,7},{7,6},{8,9},{9,8},{10,11... | collective-permute-start | bytes 24584 | tf_op jit(solution)/shard_map/ppermute | solution.py:365
  24.1 6.8 %collective-permute-start.9 = (s16[144,1024]{1,0:T(8,128)(2,1)S(1)}, s16[144,1024]{1,0:T(8,128)(2,1)S(1)}, u32[]{:S(2)}, u32[]{:S(2)}) collective-permute-start(s16[144,1024]{1,0:T(8,128)(2,1)S(1)} %shard_map.75), channel_id=1, source_target_pairs={{0,4},{1,3},{2,6},{3,1},{4,0},{5,7},{6,2},{7,5},{8,12},{9,11},{10,... | collective-permute-start | bytes 884744 | tf_op jit(solution)/shard_map/ppermute | solution.py:374
  31.3 8.4 %collective-permute-start.10 = (s16[144,256]{1,0:T(8,128)(2,1)S(1)}, s16[144,256]{1,0:T(8,128)(2,1)S(1)}, u32[]{:S(2)}, u32[]{:S(2)}) collective-permute-start(s16[144,256]{1,0:T(8,128)(2,1)S(1)} %get-tuple-element.34), channel_id=1, source_target_pairs={{0,8},{1,5},{2,10},{3,7},{4,12},{5,1},{6,14},{7,3},{8,0},{9,13},{1... | collective-permute-start | bytes 221192 | tf_op jit(solution)/shard_map/ppermute | solution.py:374
  33.5 6.2 %collective-permute-start.11 = (s16[144,256]{1,0:T(8,128)(2,1)S(1)}, s16[144,256]{1,0:T(8,128)(2,1)S(1)}, u32[]{:S(2)}, u32[]{:S(2)}) collective-permute-start(s16[144,256]{1,0:T(8,128)(2,1)S(1)} %get-tuple-element.35), channel_id=1, source_target_pairs={{0,2},{1,9},{2,0},{3,11},{4,6},{5,13},{6,4},{7,15},{8,10},{9,1},{1... | collective-permute-start | bytes 221192 | tf_op jit(solution)/shard_map/ppermute | solution.py:374
  33.8 7.6 %collective-permute-start.12 = (s16[144,256]{1,0:T(8,128)(2,1)S(1)}, s16[144,256]{1,0:T(8,128)(2,1)S(1)}, u32[]{:S(2)}, u32[]{:S(2)}) collective-permute-start(s16[144,256]{1,0:T(8,128)(2,1)S(1)} %get-tuple-element.36), channel_id=1, source_target_pairs={{0,10},{1,13},{2,8},{3,15},{4,14},{5,9},{6,12},{7,11},{8,2},{9,5},... | collective-permute-start | bytes 221192 | tf_op jit(solution)/shard_map/ppermute | solution.py:374
  41.5 1.3 %collective-permute-start.13 = (bf16[4,4096]{1,0:T(4,128)(2,1)S(1)}, bf16[4,4096]{1,0:T(4,128)(2,1)S(1)}, u32[]{:S(2)}, u32[]{:S(2)}) collective-permute-start(bf16[4,4096]{1,0:T(4,128)(2,1)S(1)} %get-tuple-element.38), channel_id=1, source_target_pairs={{0,1},{1,0},{2,3},{3,2},{4,5},{5,4},{6,7},{7,6},{8,9},{9,8},{10,11... | collective-permute-start | bytes 98312 | tf_op jit(solution)/shard_map/ppermute | solution.py:365
where the time goes:
time: 43.7 us; the launch traced here: 43.4 us
  waiting for transfers between devices  14.6 us (33%)
  starting transfers between devices  13.4 us (31%)
  Pallas kernels  11.8 us (27%)
  local copies, waits for them, and re-layouts  2.27 us (5%)
  between operations  1.41 us (3%)
    ppermute x8, waiting for transfers between devices, exchange(): lax.ppermute(x, 'ctx', [(i, i ^ distance[i % CORES]) for i in range(width)])  13.4 us
    ppermute x8, starting transfers between devices, exchange(): lax.ppermute(x, 'ctx', [(i, i ^ distance[i % CORES]) for i in range(width)])  12.1 us
    pallas_call x2, Pallas kernels, attend(): pl.pallas_call(functools.partial(attend_kernel, sizes), out_shape=jax.Sha...  9.78 us
    dynamic_slice x2, local copies, waits for them, and re-layouts, own_half(): return lax.dynamic_slice_in_dim(x, core * half, half, 1)  2.24 us
    ppermute x6, starting transfers between devices, swap(): return lax.ppermute(x, 'ctx', [(i, i ^ 1) for i in range(width)])  1.25 us
    ppermute x6, waiting for transfers between devices, swap(): return lax.ppermute(x, 'ctx', [(i, i ^ 1) for i in range(width)])  1.21 us
  transfers between devices with their start and end apart: 14, of which 7 were waited for; matrix products, arithmetic and copies ran while one was open for 5% of the time, Pallas kernels for 11%

commit v1 on v0

--- a/solution.py
+++ b/solution.py
@@ -400,7 +400,8 @@
     parts = [near, exchange(far, partners((last,))[0])]
     for stage in [(i - 1, i) if i else (i,) for i in range(last - 1, -1, -2)]:
         parts = merge(parts, 1 << len(stage))
-        parts = [parts[0]] + [exchange(x, distance) for x, distance in zip(parts[1:], partners(stage))]
+        sent = list(zip(parts[1:], partners(stage)))
+        parts = [parts[0]] + [exchange(x, distance) for x, distance in sent[1:] + sent[:1]]
     mine, other = finish(parts, own_rows, group)
     return place(mine, swap(other))
 

time: 43.7 us -> 42.8 us (0.979); the launches traced: 43.4 us -> 42 us
  Pallas kernels: 11.8 us -> 9.14 us
  starting transfers between devices: 13.4 us -> 15.5 us
  waiting for transfers between devices: 14.6 us -> 13.7 us
    pallas_call x2, Pallas kernels: 9.78 us -> 7.16 us  [attend(): pl.pallas_call(functools.partial(attend_kernel, sizes), out_shape=jax.Sha...]
    ppermute x8, starting transfers between devices: 12.1 us -> 14.2 us  [exchange(): lax.ppermute(x, 'ctx', [(i, i ^ distance[i % CORES]) for i in range(width)])]
    ppermute x8, waiting for transfers between devices: 13.4 us -> 12.5 us  [exchange(): lax.ppermute(x, 'ctx', [(i, i ^ distance[i % CORES]) for i in range(width)])]
  transfers between devices with their start and end apart: 14 -> 14, of which waited for: 7 -> 7; matrix products, arithmetic and copies ran while one was open for 5% -> 5% of each run, Pallas kernels for 11% -> 9%
where the time goes in v1:
time: 42.8 us; the launch traced here: 42 us
  starting transfers between devices  15.5 us (36%)
  waiting for transfers between devices  13.7 us (32%)
  Pallas kernels  9.14 us (21%)
  local copies, waits for them, and re-layouts  2.27 us (5%)
  between operations  1.4 us (3%)
    ppermute x8, starting transfers between devices, exchange(): lax.ppermute(x, 'ctx', [(i, i ^ distance[i % CORES]) for i in range(width)])  14.2 us
    ppermute x8, waiting for transfers between devices, exchange(): lax.ppermute(x, 'ctx', [(i, i ^ distance[i % CORES]) for i in range(width)])  12.5 us
    pallas_call x2, Pallas kernels, attend(): pl.pallas_call(functools.partial(attend_kernel, sizes), out_shape=jax.Sha...  7.16 us
    dynamic_slice x2, local copies, waits for them, and re-layouts, own_half(): return lax.dynamic_slice_in_dim(x, core * half, half, 1)  2.24 us
    ppermute x6, starting transfers between devices, swap(): return lax.ppermute(x, 'ctx', [(i, i ^ 1) for i in range(width)])  1.25 us
    ppermute x6, waiting for transfers between devices, swap(): return lax.ppermute(x, 'ctx', [(i, i ^ 1) for i in range(width)])  1.21 us
  transfers between devices with their start and end apart: 14, of which 7 were waited for; matrix products, arithmetic and copies ran while one was open for 5% of the time, Pallas kernels for 9%

profile of v1, /device:TPU:0, one launch (start us, length us, event | category | flops | bytes accessed | tf_op | source)
XLA Modules:
  0.0 42.0 jit_solution(15131789957994765211)
XLA Ops:
  0.0 0.5 %collective-permute-start = (s32[1]{0:T(128)}, s32[1]{0:T(128)}, u32[]{:S(2)}, u32[]{:S(2)}) collective-permute-start(s32[1]{0:T(128)} %param.12), channel_id=1, source_target_pairs={{0,1},{1,0},{2,3},{3,2},{4,5},{5,4},{6,7},{7,6},{8,9},{9,8},{10,11... | collective-permute-start | bytes 20 | tf_op jit(solution)/shard_map/ppermute | solution.py:365
  0.5 0.1 collective-permute-start.1
  0.5 0.8 %constant_dynamic-slice_fusion.2.mine = bf16[4,4096]{1,0:T(4,128)(2,1)S(1)} fusion(bf16[4,8192]{1,0:T(4,128)(2,1)} %param.7, s32[]{:T(128)S(6)} %select_n.15), kind=kLoop, calls=%fused_computation.5 | loop fusion | bytes 65540 | tf_op jit(solution)/shard_map/dynamic_slice | solution.py:378
  1.9 0.0 collective-permute-done.length_other
  1.9 0.0 collective-permute-done.1.queries_other
  2.0 0.7 %shard_map.73 = bf16[8,4224]{1,0:T(8,128)(2,1)S(1)} custom-call(s32[1]{0:T(128)S(6)} %copy.9.length, s32[1]{0:T(128)} %collective-permute-done.length_other, bf16[4,4096]{1,0:T(4,128)(2,1)S(1)} %constant_dynamic-slice_fusion.2.mine, bf16[4,8192]{1,0:T(4,128)(2,1)S(1)} %collective-permute-done.1.queries_other), custom_call_target="tpu_custom_call" | custom-call | tf_op jit(solution)/shard_map/pallas_call | solution.py:86
  2.7 0.5 %collective-permute-start.7 = (bf16[1536,512]{1,0:T(8,128)(2,1)}, bf16[1536,512]{1,0:T(8,128)(2,1)S(1)}, u32[]{:S(2)}, u32[]{:S(2)}) collective-permute-start(bf16[1536,512]{1,0:T(8,128)(2,1)} %param.8), channel_id=1, source_target_pairs={{0,1},{1,0},{2,3},{3,2},{4,5},{5,4},{6,7},{7,6},{8,9},{9,8},{10,11... | collective-permute-start | bytes 4718600 | tf_op jit(solution)/shard_map/ppermute | solution.py:365
  3.2 0.1 collective-permute-start.8
  3.3 4.0 %collective-permute-start.2 = (bf16[8,4224]{1,0:T(8,128)(2,1)S(1)}, bf16[8,4224]{1,0:T(8,128)(2,1)S(1)}, u32[]{:S(2)}, u32[]{:S(2)}) collective-permute-start(bf16[8,4224]{1,0:T(8,128)(2,1)S(1)} %shard_map.73), channel_id=1, source_target_pairs={{0,8},{1,5},{2,10},{3,7},{4,12},{5,1},{6,14},{7,3},{8,0},{9,13},{1... | collective-permute-start | bytes 202760 | tf_op jit(solution)/shard_map/ppermute | solution.py:374
  7.3 2.3 %collective-permute-done.2 = bf16[8,4224]{1,0:T(8,128)(2,1)S(1)} collective-permute-done((bf16[8,4224]{1,0:T(8,128)(2,1)S(1)}, bf16[8,4224]{1,0:T(8,128)(2,1)S(1)}, u32[]{:S(2)}, u32[]{:S(2)}) %collective-permute-start.2) | collective-permute-done | bytes 67616 | tf_op jit(solution)/shard_map/ppermute | solution.py:374
  9.6 0.0 copy-start
  9.6 0.0 copy-start.1
  9.6 2.9 %collective-permute-start.5 = (bf16[16,4224]{1,0:T(8,128)(2,1)S(1)}, bf16[16,4224]{1,0:T(8,128)(2,1)S(1)}, u32[]{:S(2)}, u32[]{:S(2)}) collective-permute-start(bf16[16,4224]{1,0:T(8,128)(2,1)S(1)} %constant_dynamic-update-slice_fusion.refs_1_), channel_id=1, source_target_pairs={{0,6},{1,11},{2,4},{3,9},{4,2},{5,15},{6,0},{7,13},{8,14},{9,3},{1... | collective-permute-start | bytes 405512 | tf_op jit(solution)/shard_map/ppermute | solution.py:374
  12.5 0.4 %collective-permute-start.4 = (bf16[16,4224]{1,0:T(8,128)(2,1)S(1)}, bf16[16,4224]{1,0:T(8,128)(2,1)S(1)}, u32[]{:S(2)}, u32[]{:S(2)}) collective-permute-start(bf16[16,4224]{1,0:T(8,128)(2,1)S(1)} %constant_dynamic-update-slice_fusion.refs_1_), channel_id=1, source_target_pairs={{0,4},{1,3},{2,6},{3,1},{4,0},{5,7},{6,2},{7,5},{8,12},{9,11},{10,... | collective-permute-start | bytes 405512 | tf_op jit(solution)/shard_map/ppermute | solution.py:374
  13.0 0.2 collective-permute-start.3
  13.2 1.5 %constant_dynamic-slice_fusion = (bf16[1536,256]{1,0:T(8,128)(2,1)S(1)}, bf16[1536,256]{1,0:T(8,128)(2,1)S(1)}) fusion(bf16[1536,512]{1,0:T(8,128)(2,1)} %param.9, s32[]{:T(128)S(6)} %select_n.16, bf16[1536,512]{1,0:T(8,128)(2,1)} %param.8), kind=kLoop, calls=%fused_computation.3 | loop fusion | bytes 3145732 | tf_op jit(solution)/shard_map/dynamic_slice | solution.py:378
  14.6 1.4 %collective-permute-done.5.refs_4_ = bf16[16,4224]{1,0:T(8,128)(2,1)S(1)} collective-permute-done((bf16[16,4224]{1,0:T(8,128)(2,1)S(1)}, bf16[16,4224]{1,0:T(8,128)(2,1)S(1)}, u32[]{:S(2)}, u32[]{:S(2)}) %collective-permute-start.5) | collective-permute-done | bytes 135200 | tf_op jit(solution)/shard_map/ppermute | solution.py:374
  16.0 0.0 copy-done
  16.1 0.0 copy-done.1
  16.1 0.1 collective-permute-start.6
  16.8 2.4 %collective-permute-done.4.refs_3_ = bf16[16,4224]{1,0:T(8,128)(2,1)S(1)} collective-permute-done((bf16[16,4224]{1,0:T(8,128)(2,1)S(1)}, bf16[16,4224]{1,0:T(8,128)(2,1)S(1)}, u32[]{:S(2)}, u32[]{:S(2)}) %collective-permute-start.4) | collective-permute-done | bytes 135200 | tf_op jit(solution)/shard_map/ppermute | solution.py:374
  19.2 0.0 collective-permute-done.3.refs_2_
  19.2 0.0 collective-permute-done.6.refs_6_
  19.2 0.0 collective-permute-done.7.refs_8_
  19.2 0.0 collective-permute-done.8.refs_10_
  19.2 3.6 %shard_map.75 = s16[144,1024]{1,0:T(8,128)(2,1)S(1)} custom-call(s32[1]{0:T(128)S(6)} %copy.10.refs_0_, bf16[16,4224]{1,0:T(8,128)(2,1)S(1)} %constant_dynamic-update-slice_fusion.refs_1_, bf16[16,4224]{1,0:T(8,128)(2,1)S(1)} %collective-permute-done.3.refs_2_, bf16[16,4224]{1,0:T(8,128)(2,1)S(1)} %collective-permute-done.4.refs_3_, ...), custom_call_target="tpu_custom_call" | custom-call | tf_op jit(solution)/shard_map/pallas_call | solution.py:258
  22.8 2.2 %collective-permute-start.9 = (s16[144,1024]{1,0:T(8,128)(2,1)S(1)}, s16[144,1024]{1,0:T(8,128)(2,1)S(1)}, u32[]{:S(2)}, u32[]{:S(2)}) collective-permute-start(s16[144,1024]{1,0:T(8,128)(2,1)S(1)} %shard_map.75), channel_id=1, source_target_pairs={{0,4},{1,3},{2,6},{3,1},{4,0},{5,7},{6,2},{7,5},{8,12},{9,11},{10,... | collective-permute-start | bytes 884744 | tf_op jit(solution)/shard_map/ppermute | solution.py:374
  24.9 3.6 %shard_map.74.refs_0_ = s16[144,1024]{1,0:T(8,128)(2,1)S(1)} custom-call(s32[1]{0:T(128)S(6)} %copy.10.refs_0_, bf16[16,4224]{1,0:T(8,128)(2,1)S(1)} %constant_dynamic-update-slice_fusion.refs_1_, bf16[16,4224]{1,0:T(8,128)(2,1)S(1)} %collective-permute-done.3.refs_2_, bf16[16,4224]{1,0:T(8,128)(2,1)S(1)} %collective-permute-done.4.refs_3_, ...), custom_call_target="tpu_custom_call" | custom-call | tf_op jit(solution)/shard_map/pallas_call | solution.py:258
  28.6 1.1 %collective-permute-done.9.refs_1_ = s16[144,1024]{1,0:T(8,128)(2,1)S(1)} collective-permute-done((s16[144,1024]{1,0:T(8,128)(2,1)S(1)}, s16[144,1024]{1,0:T(8,128)(2,1)S(1)}, u32[]{:S(2)}, u32[]{:S(2)}) %collective-permute-start.9) | collective-permute-done | bytes 294944 | tf_op jit(solution)/shard_map/ppermute | solution.py:374
  29.6 0.4 %shard_map.76 = (s16[144,256]{1,0:T(8,128)(2,1)S(1)}, s16[144,256]{1,0:T(8,128)(2,1)S(1)}, s16[144,256]{1,0:T(8,128)(2,1)S(1)}, s16[144,256]{1,0:T(8,128)(2,1)S(1)}) custom-call(s16[144,1024]{1,0:T(8,128)(2,1)S(1)} %shard_map.74.refs_0_, s16[144,1024]{1,0:T(8,128)(2,1)S(1)} %collective-permute-done.9.refs_1_), custom_call_target="tpu_custom_call" | custom-call | tf_op jit(solution)/shard_map/pallas_call | solution.py:298
  30.1 0.5 %collective-permute-start.10 = (s16[144,256]{1,0:T(8,128)(2,1)S(1)}, s16[144,256]{1,0:T(8,128)(2,1)S(1)}, u32[]{:S(2)}, u32[]{:S(2)}) collective-permute-start(s16[144,256]{1,0:T(8,128)(2,1)S(1)} %get-tuple-element.34), channel_id=1, source_target_pairs={{0,2},{1,9},{2,0},{3,11},{4,6},{5,13},{6,4},{7,15},{8,10},{9,1},{1... | collective-permute-start | bytes 221192 | tf_op jit(solution)/shard_map/ppermute | solution.py:374
  30.6 2.9 %collective-permute-start.11 = (s16[144,256]{1,0:T(8,128)(2,1)S(1)}, s16[144,256]{1,0:T(8,128)(2,1)S(1)}, u32[]{:S(2)}, u32[]{:S(2)}) collective-permute-start(s16[144,256]{1,0:T(8,128)(2,1)S(1)} %get-tuple-element.35), channel_id=1, source_target_pairs={{0,10},{1,13},{2,8},{3,15},{4,14},{5,9},{6,12},{7,11},{8,2},{9,5},... | collective-permute-start | bytes 221192 | tf_op jit(solution)/shard_map/ppermute | solution.py:374
  33.5 1.0 %collective-permute-start.12 = (s16[144,256]{1,0:T(8,128)(2,1)S(1)}, s16[144,256]{1,0:T(8,128)(2,1)S(1)}, u32[]{:S(2)}, u32[]{:S(2)}) collective-permute-start(s16[144,256]{1,0:T(8,128)(2,1)S(1)} %get-tuple-element.36), channel_id=1, source_target_pairs={{0,8},{1,5},{2,10},{3,7},{4,12},{5,1},{6,14},{7,3},{8,0},{9,13},{1... | collective-permute-start | bytes 221192 | tf_op jit(solution)/shard_map/ppermute | solution.py:374
  34.5 0.0 collective-permute-done.10.refs_1_
  34.5 3.6 %collective-permute-done.11.refs_2_ = s16[144,256]{1,0:T(8,128)(2,1)S(1)} collective-permute-done((s16[144,256]{1,0:T(8,128)(2,1)S(1)}, s16[144,256]{1,0:T(8,128)(2,1)S(1)}, u32[]{:S(2)}, u32[]{:S(2)}) %collective-permute-start.11) | collective-permute-done | bytes 73760 | tf_op jit(solution)/shard_map/ppermute | solution.py:374
  38.2 1.7 %collective-permute-done.12.refs_3_ = s16[144,256]{1,0:T(8,128)(2,1)S(1)} collective-permute-done((s16[144,256]{1,0:T(8,128)(2,1)S(1)}, s16[144,256]{1,0:T(8,128)(2,1)S(1)}, u32[]{:S(2)}, u32[]{:S(2)}) %collective-permute-start.12) | collective-permute-done | bytes 73760 | tf_op jit(solution)/shard_map/ppermute | solution.py:374
  39.9 0.2 shard_map.77
  40.1 0.1 collective-permute-start.13
  40.2 1.2 %collective-permute-done.13.theirs = bf16[4,4096]{1,0:T(4,128)(2,1)S(1)} collective-permute-done((bf16[4,4096]{1,0:T(4,128)(2,1)S(1)}, bf16[4,4096]{1,0:T(4,128)(2,1)S(1)}, u32[]{:S(2)}, u32[]{:S(2)}) %collective-permute-start.13) | collective-permute-done | bytes 32800 | tf_op jit(solution)/shard_map/ppermute | solution.py:365
  41.4 0.6 %shard_map.78 = bf16[4,8192]{1,0:T(4,128)(2,1)} custom-call(bf16[4,4096]{1,0:T(4,128)(2,1)S(1)} %get-tuple-element.37.mine, bf16[4,4096]{1,0:T(4,128)(2,1)S(1)} %collective-permute-done.13.theirs), custom_call_target="tpu_custom_call" | custom-call | tf_op jit(solution)/shard_map/pallas_call | solution.py:344
  (3 shorter events, 0.0 us)
Async XLA Ops:
  0.0 1.9 %collective-permute-start = (s32[1]{0:T(128)}, s32[1]{0:T(128)}, u32[]{:S(2)}, u32[]{:S(2)}) collective-permute-start(s32[1]{0:T(128)} %param.12), channel_id=1, source_target_pairs={{0,1},{1,0},{2,3},{3,2},{4,5},{5,4},{6,7},{7,6},{8,9},{9,8},{10,11... | collective-permute-start | bytes 20 | tf_op jit(solution)/shard_map/ppermute | solution.py:365
  0.5 1.5 %collective-permute-start.1 = (bf16[4,8192]{1,0:T(4,128)(2,1)}, bf16[4,8192]{1,0:T(4,128)(2,1)S(1)}, u32[]{:S(2)}, u32[]{:S(2)}) collective-permute-start(bf16[4,8192]{1,0:T(4,128)(2,1)} %param.7), channel_id=1, source_target_pairs={{0,1},{1,0},{2,3},{3,2},{4,5},{5,4},{6,7},{7,6},{8,9},{9,8},{10,11... | collective-permute-start | bytes 196616 | tf_op jit(solution)/shard_map/ppermute | solution.py:365
  2.7 16.5 %collective-permute-start.7 = (bf16[1536,512]{1,0:T(8,128)(2,1)}, bf16[1536,512]{1,0:T(8,128)(2,1)S(1)}, u32[]{:S(2)}, u32[]{:S(2)}) collective-permute-start(bf16[1536,512]{1,0:T(8,128)(2,1)} %param.8), channel_id=1, source_target_pairs={{0,1},{1,0},{2,3},{3,2},{4,5},{5,4},{6,7},{7,6},{8,9},{9,8},{10,11... | collective-permute-start | bytes 4718600 | tf_op jit(solution)/shard_map/ppermute | solution.py:365
  3.2 16.0 %collective-permute-start.8 = (bf16[1536,512]{1,0:T(8,128)(2,1)}, bf16[1536,512]{1,0:T(8,128)(2,1)S(1)}, u32[]{:S(2)}, u32[]{:S(2)}) collective-permute-start(bf16[1536,512]{1,0:T(8,128)(2,1)} %param.9), channel_id=1, source_target_pairs={{0,1},{1,0},{2,3},{3,2},{4,5},{5,4},{6,7},{7,6},{8,9},{9,8},{10,11... | collective-permute-start | bytes 4718600 | tf_op jit(solution)/shard_map/ppermute | solution.py:365
  3.3 6.3 %collective-permute-start.2 = (bf16[8,4224]{1,0:T(8,128)(2,1)S(1)}, bf16[8,4224]{1,0:T(8,128)(2,1)S(1)}, u32[]{:S(2)}, u32[]{:S(2)}) collective-permute-start(bf16[8,4224]{1,0:T(8,128)(2,1)S(1)} %shard_map.73), channel_id=1, source_target_pairs={{0,8},{1,5},{2,10},{3,7},{4,12},{5,1},{6,14},{7,3},{8,0},{9,13},{1... | collective-permute-start | bytes 202760 | tf_op jit(solution)/shard_map/ppermute | solution.py:374
  9.6 6.5 %copy-start = (bf16[4,512]{1,0:T(4,128)(2,1)S(1)}, bf16[4,512]{1,0:T(4,128)(2,1)}, u32[]{:S(2)}) copy-start(bf16[4,512]{1,0:T(4,128)(2,1)} %param.11) | copy-start | bytes 12292
  9.6 6.5 %copy-start.1 = (bf16[4,512]{1,0:T(4,128)(2,1)S(1)}, bf16[4,512]{1,0:T(4,128)(2,1)}, u32[]{:S(2)}) copy-start(bf16[4,512]{1,0:T(4,128)(2,1)} %param.10) | copy-start | bytes 12292
  9.6 6.5 %collective-permute-start.5 = (bf16[16,4224]{1,0:T(8,128)(2,1)S(1)}, bf16[16,4224]{1,0:T(8,128)(2,1)S(1)}, u32[]{:S(2)}, u32[]{:S(2)}) collective-permute-start(bf16[16,4224]{1,0:T(8,128)(2,1)S(1)} %constant_dynamic-update-slice_fusion.refs_1_), channel_id=1, source_target_pairs={{0,6},{1,11},{2,4},{3,9},{4,2},{5,15},{6,0},{7,13},{8,14},{9,3},{1... | collective-permute-start | bytes 405512 | tf_op jit(solution)/shard_map/ppermute | solution.py:374
  12.5 6.7 %collective-permute-start.4 = (bf16[16,4224]{1,0:T(8,128)(2,1)S(1)}, bf16[16,4224]{1,0:T(8,128)(2,1)S(1)}, u32[]{:S(2)}, u32[]{:S(2)}) collective-permute-start(bf16[16,4224]{1,0:T(8,128)(2,1)S(1)} %constant_dynamic-update-slice_fusion.refs_1_), channel_id=1, source_target_pairs={{0,4},{1,3},{2,6},{3,1},{4,0},{5,7},{6,2},{7,5},{8,12},{9,11},{10,... | collective-permute-start | bytes 405512 | tf_op jit(solution)/shard_map/ppermute | solution.py:374
  13.0 6.2 %collective-permute-start.3 = (bf16[16,4224]{1,0:T(8,128)(2,1)S(1)}, bf16[16,4224]{1,0:T(8,128)(2,1)S(1)}, u32[]{:S(2)}, u32[]{:S(2)}) collective-permute-start(bf16[16,4224]{1,0:T(8,128)(2,1)S(1)} %constant_dynamic-update-slice_fusion.refs_1_), channel_id=1, source_target_pairs={{0,2},{1,9},{2,0},{3,11},{4,6},{5,13},{6,4},{7,15},{8,10},{9,1},{1... | collective-permute-start | bytes 405512 | tf_op jit(solution)/shard_map/ppermute | solution.py:374
  16.1 3.1 %collective-permute-start.6 = (bf16[8,512]{1,0:T(8,128)(2,1)S(1)}, bf16[8,512]{1,0:T(8,128)(2,1)S(1)}, u32[]{:S(2)}, u32[]{:S(2)}) collective-permute-start(bf16[8,512]{1,0:T(8,128)(2,1)S(1)} %pad_maximum_fusion.refs_5_), channel_id=1, source_target_pairs={{0,1},{1,0},{2,3},{3,2},{4,5},{5,4},{6,7},{7,6},{8,9},{9,8},{10,11... | collective-permute-start | bytes 24584 | tf_op jit(solution)/shard_map/ppermute | solution.py:365
  22.8 6.9 %collective-permute-start.9 = (s16[144,1024]{1,0:T(8,128)(2,1)S(1)}, s16[144,1024]{1,0:T(8,128)(2,1)S(1)}, u32[]{:S(2)}, u32[]{:S(2)}) collective-permute-start(s16[144,1024]{1,0:T(8,128)(2,1)S(1)} %shard_map.75), channel_id=1, source_target_pairs={{0,4},{1,3},{2,6},{3,1},{4,0},{5,7},{6,2},{7,5},{8,12},{9,11},{10,... | collective-permute-start | bytes 884744 | tf_op jit(solution)/shard_map/ppermute | solution.py:374
  30.1 4.5 %collective-permute-start.10 = (s16[144,256]{1,0:T(8,128)(2,1)S(1)}, s16[144,256]{1,0:T(8,128)(2,1)S(1)}, u32[]{:S(2)}, u32[]{:S(2)}) collective-permute-start(s16[144,256]{1,0:T(8,128)(2,1)S(1)} %get-tuple-element.34), channel_id=1, source_target_pairs={{0,2},{1,9},{2,0},{3,11},{4,6},{5,13},{6,4},{7,15},{8,10},{9,1},{1... | collective-permute-start | bytes 221192 | tf_op jit(solution)/shard_map/ppermute | solution.py:374
  30.6 7.6 %collective-permute-start.11 = (s16[144,256]{1,0:T(8,128)(2,1)S(1)}, s16[144,256]{1,0:T(8,128)(2,1)S(1)}, u32[]{:S(2)}, u32[]{:S(2)}) collective-permute-start(s16[144,256]{1,0:T(8,128)(2,1)S(1)} %get-tuple-element.35), channel_id=1, source_target_pairs={{0,10},{1,13},{2,8},{3,15},{4,14},{5,9},{6,12},{7,11},{8,2},{9,5},... | collective-permute-start | bytes 221192 | tf_op jit(solution)/shard_map/ppermute | solution.py:374
  33.5 6.4 %collective-permute-start.12 = (s16[144,256]{1,0:T(8,128)(2,1)S(1)}, s16[144,256]{1,0:T(8,128)(2,1)S(1)}, u32[]{:S(2)}, u32[]{:S(2)}) collective-permute-start(s16[144,256]{1,0:T(8,128)(2,1)S(1)} %get-tuple-element.36), channel_id=1, source_target_pairs={{0,8},{1,5},{2,10},{3,7},{4,12},{5,1},{6,14},{7,3},{8,0},{9,13},{1... | collective-permute-start | bytes 221192 | tf_op jit(solution)/shard_map/ppermute | solution.py:374
  40.1 1.3 %collective-permute-start.13 = (bf16[4,4096]{1,0:T(4,128)(2,1)S(1)}, bf16[4,4096]{1,0:T(4,128)(2,1)S(1)}, u32[]{:S(2)}, u32[]{:S(2)}) collective-permute-start(bf16[4,4096]{1,0:T(4,128)(2,1)S(1)} %get-tuple-element.38), channel_id=1, source_target_pairs={{0,1},{1,0},{2,3},{3,2},{4,5},{5,4},{6,7},{7,6},{8,9},{9,8},{10,11... | collective-permute-start | bytes 98312 | tf_op jit(solution)/shard_map/ppermute | solution.py:365

commit v2 on v1

--- a/solution.py
+++ b/solution.py
@@ -382,7 +382,9 @@
     cache_keys, cached_value_rows, held = lax.optimization_barrier((cache_keys, cached_value_rows, held))
     cache = [y for x in (cache_keys, cached_value_rows) for y in (own_half(x), swap(x))]
     for stage in stages:
-        gathered = [held] + [exchange(held, distance) for distance in partners(stage)]
+        distances = partners(stage)
+        came = [exchange(held, distance) for distance in distances[1:] + distances[:1]]
+        gathered = [held] + came[-1:] + came[:-1]
         if stage != stages[-1]:
             held = jnp.concatenate(gathered, axis=0)
     cache[0], cache[2], prompt_start = lax.optimization_barrier((cache[0], cache[2], prompt_start))

time: 42.8 us -> 42.4 us (level)
  Pallas kernels: 9.14 us -> 11.2 us
  starting transfers between devices: 15.5 us -> 14.4 us
  waiting for transfers between devices: 13.7 us -> 12.6 us
    pallas_call x2, Pallas kernels: 7.16 us -> 9.23 us  [attend(): pl.pallas_call(functools.partial(attend_kernel, sizes), out_shape=jax.Sha...]
    ppermute x8, waiting for transfers between devices: 12.5 us -> 11.4 us  [exchange(): lax.ppermute(x, 'ctx', [(i, i ^ distance[i % CORES]) for i in range(width)])]
    ppermute x8, starting transfers between devices: 14.2 us -> 13.2 us  [exchange(): lax.ppermute(x, 'ctx', [(i, i ^ distance[i % CORES]) for i in range(width)])]
  transfers between devices with their start and end apart: 14 -> 14, of which waited for: 7 -> 7; matrix products, arithmetic and copies ran while one was open for 5% -> 5% of each run, Pallas kernels for 9% -> 11%
where the time goes in v2:
time: 42.4 us; the launch traced here: 41.9 us
  starting transfers between devices  14.4 us (34%)
  waiting for transfers between devices  12.6 us (30%)
  Pallas kernels  11.2 us (26%)
  local copies, waits for them, and re-layouts  2.27 us (5%)
  between operations  1.4 us (3%)
    ppermute x8, starting transfers between devices, exchange(): lax.ppermute(x, 'ctx', [(i, i ^ distance[i % CORES]) for i in range(width)])  13.2 us
    ppermute x8, waiting for transfers between devices, exchange(): lax.ppermute(x, 'ctx', [(i, i ^ distance[i % CORES]) for i in range(width)])  11.4 us
    pallas_call x2, Pallas kernels, attend(): pl.pallas_call(functools.partial(attend_kernel, sizes), out_shape=jax.Sha...  9.23 us
    dynamic_slice x2, local copies, waits for them, and re-layouts, own_half(): return lax.dynamic_slice_in_dim(x, core * half, half, 1)  2.24 us
    ppermute x6, starting transfers between devices, swap(): return lax.ppermute(x, 'ctx', [(i, i ^ 1) for i in range(width)])  1.25 us
    ppermute x6, waiting for transfers between devices, swap(): return lax.ppermute(x, 'ctx', [(i, i ^ 1) for i in range(width)])  1.21 us
  transfers between devices with their start and end apart: 14, of which 7 were waited for; matrix products, arithmetic and copies ran while one was open for 5% of the time, Pallas kernels for 11%

profile of v2, /device:TPU:0, one launch (start us, length us, event | category | flops | bytes accessed | tf_op | source)
XLA Modules:
  0.0 41.9 jit_solution(15131789957994765211)
XLA Ops:
  0.0 0.5 %collective-permute-start = (s32[1]{0:T(128)}, s32[1]{0:T(128)}, u32[]{:S(2)}, u32[]{:S(2)}) collective-permute-start(s32[1]{0:T(128)} %param.12), channel_id=1, source_target_pairs={{0,1},{1,0},{2,3},{3,2},{4,5},{5,4},{6,7},{7,6},{8,9},{9,8},{10,11... | collective-permute-start | bytes 20 | tf_op jit(solution)/shard_map/ppermute | solution.py:365
  0.5 0.1 collective-permute-start.1
  0.5 0.8 %constant_dynamic-slice_fusion.2.mine = bf16[4,4096]{1,0:T(4,128)(2,1)S(1)} fusion(bf16[4,8192]{1,0:T(4,128)(2,1)} %param.7, s32[]{:T(128)S(6)} %select_n.15), kind=kLoop, calls=%fused_computation.5 | loop fusion | bytes 65540 | tf_op jit(solution)/shard_map/dynamic_slice | solution.py:378
  1.9 0.0 collective-permute-done.length_other
  1.9 0.0 collective-permute-done.1.queries_other
  2.0 0.7 %shard_map.73 = bf16[8,4224]{1,0:T(8,128)(2,1)S(1)} custom-call(s32[1]{0:T(128)S(6)} %copy.9.length, s32[1]{0:T(128)} %collective-permute-done.length_other, bf16[4,4096]{1,0:T(4,128)(2,1)S(1)} %constant_dynamic-slice_fusion.2.mine, bf16[4,8192]{1,0:T(4,128)(2,1)S(1)} %collective-permute-done.1.queries_other), custom_call_target="tpu_custom_call" | custom-call | tf_op jit(solution)/shard_map/pallas_call | solution.py:86
  2.7 0.5 %collective-permute-start.7 = (bf16[1536,512]{1,0:T(8,128)(2,1)}, bf16[1536,512]{1,0:T(8,128)(2,1)S(1)}, u32[]{:S(2)}, u32[]{:S(2)}) collective-permute-start(bf16[1536,512]{1,0:T(8,128)(2,1)} %param.8), channel_id=1, source_target_pairs={{0,1},{1,0},{2,3},{3,2},{4,5},{5,4},{6,7},{7,6},{8,9},{9,8},{10,11... | collective-permute-start | bytes 4718600 | tf_op jit(solution)/shard_map/ppermute | solution.py:365
  3.2 0.1 collective-permute-start.8
  3.3 4.0 %collective-permute-start.2 = (bf16[8,4224]{1,0:T(8,128)(2,1)S(1)}, bf16[8,4224]{1,0:T(8,128)(2,1)S(1)}, u32[]{:S(2)}, u32[]{:S(2)}) collective-permute-start(bf16[8,4224]{1,0:T(8,128)(2,1)S(1)} %shard_map.73), channel_id=1, source_target_pairs={{0,8},{1,5},{2,10},{3,7},{4,12},{5,1},{6,14},{7,3},{8,0},{9,13},{1... | collective-permute-start | bytes 202760 | tf_op jit(solution)/shard_map/ppermute | solution.py:374
  7.3 2.3 %collective-permute-done.2 = bf16[8,4224]{1,0:T(8,128)(2,1)S(1)} collective-permute-done((bf16[8,4224]{1,0:T(8,128)(2,1)S(1)}, bf16[8,4224]{1,0:T(8,128)(2,1)S(1)}, u32[]{:S(2)}, u32[]{:S(2)}) %collective-permute-start.2) | collective-permute-done | bytes 67616 | tf_op jit(solution)/shard_map/ppermute | solution.py:374
  9.6 0.0 copy-start
  9.6 0.0 copy-start.1
  9.6 2.9 %collective-permute-start.5 = (bf16[16,4224]{1,0:T(8,128)(2,1)S(1)}, bf16[16,4224]{1,0:T(8,128)(2,1)S(1)}, u32[]{:S(2)}, u32[]{:S(2)}) collective-permute-start(bf16[16,4224]{1,0:T(8,128)(2,1)S(1)} %constant_dynamic-update-slice_fusion.refs_1_), channel_id=1, source_target_pairs={{0,6},{1,11},{2,4},{3,9},{4,2},{5,15},{6,0},{7,13},{8,14},{9,3},{1... | collective-permute-start | bytes 405512 | tf_op jit(solution)/shard_map/ppermute | solution.py:374
  12.5 0.4 %collective-permute-start.4 = (bf16[16,4224]{1,0:T(8,128)(2,1)S(1)}, bf16[16,4224]{1,0:T(8,128)(2,1)S(1)}, u32[]{:S(2)}, u32[]{:S(2)}) collective-permute-start(bf16[16,4224]{1,0:T(8,128)(2,1)S(1)} %constant_dynamic-update-slice_fusion.refs_1_), channel_id=1, source_target_pairs={{0,4},{1,3},{2,6},{3,1},{4,0},{5,7},{6,2},{7,5},{8,12},{9,11},{10,... | collective-permute-start | bytes 405512 | tf_op jit(solution)/shard_map/ppermute | solution.py:374
  13.0 0.2 collective-permute-start.3
  13.2 1.5 %constant_dynamic-slice_fusion = (bf16[1536,256]{1,0:T(8,128)(2,1)S(1)}, bf16[1536,256]{1,0:T(8,128)(2,1)S(1)}) fusion(bf16[1536,512]{1,0:T(8,128)(2,1)} %param.9, s32[]{:T(128)S(6)} %select_n.16, bf16[1536,512]{1,0:T(8,128)(2,1)} %param.8), kind=kLoop, calls=%fused_computation.3 | loop fusion | bytes 3145732 | tf_op jit(solution)/shard_map/dynamic_slice | solution.py:378
  14.6 1.4 %collective-permute-done.5.refs_4_ = bf16[16,4224]{1,0:T(8,128)(2,1)S(1)} collective-permute-done((bf16[16,4224]{1,0:T(8,128)(2,1)S(1)}, bf16[16,4224]{1,0:T(8,128)(2,1)S(1)}, u32[]{:S(2)}, u32[]{:S(2)}) %collective-permute-start.5) | collective-permute-done | bytes 135200 | tf_op jit(solution)/shard_map/ppermute | solution.py:374
  16.0 0.0 copy-done
  16.1 0.0 copy-done.1
  16.1 0.1 collective-permute-start.6
  16.8 2.4 %collective-permute-done.4.refs_3_ = bf16[16,4224]{1,0:T(8,128)(2,1)S(1)} collective-permute-done((bf16[16,4224]{1,0:T(8,128)(2,1)S(1)}, bf16[16,4224]{1,0:T(8,128)(2,1)S(1)}, u32[]{:S(2)}, u32[]{:S(2)}) %collective-permute-start.4) | collective-permute-done | bytes 135200 | tf_op jit(solution)/shard_map/ppermute | solution.py:374
  19.2 0.0 collective-permute-done.3.refs_2_
  19.2 0.0 collective-permute-done.6.refs_6_
  19.2 0.0 collective-permute-done.7.refs_8_
  19.2 0.0 collective-permute-done.8.refs_10_
  19.2 4.6 %shard_map.75 = s16[144,1024]{1,0:T(8,128)(2,1)S(1)} custom-call(s32[1]{0:T(128)S(6)} %copy.10.refs_0_, bf16[16,4224]{1,0:T(8,128)(2,1)S(1)} %constant_dynamic-update-slice_fusion.refs_1_, bf16[16,4224]{1,0:T(8,128)(2,1)S(1)} %collective-permute-done.3.refs_2_, bf16[16,4224]{1,0:T(8,128)(2,1)S(1)} %collective-permute-done.4.refs_3_, ...), custom_call_target="tpu_custom_call" | custom-call | tf_op jit(solution)/shard_map/pallas_call | solution.py:258
  23.8 1.1 %collective-permute-start.9 = (s16[144,1024]{1,0:T(8,128)(2,1)S(1)}, s16[144,1024]{1,0:T(8,128)(2,1)S(1)}, u32[]{:S(2)}, u32[]{:S(2)}) collective-permute-start(s16[144,1024]{1,0:T(8,128)(2,1)S(1)} %shard_map.75), channel_id=1, source_target_pairs={{0,4},{1,3},{2,6},{3,1},{4,0},{5,7},{6,2},{7,5},{8,12},{9,11},{10,... | collective-permute-start | bytes 884744 | tf_op jit(solution)/shard_map/ppermute | solution.py:374
  24.9 4.6 %shard_map.74.refs_0_ = s16[144,1024]{1,0:T(8,128)(2,1)S(1)} custom-call(s32[1]{0:T(128)S(6)} %copy.10.refs_0_, bf16[16,4224]{1,0:T(8,128)(2,1)S(1)} %constant_dynamic-update-slice_fusion.refs_1_, bf16[16,4224]{1,0:T(8,128)(2,1)S(1)} %collective-permute-done.3.refs_2_, bf16[16,4224]{1,0:T(8,128)(2,1)S(1)} %collective-permute-done.4.refs_3_, ...), custom_call_target="tpu_custom_call" | custom-call | tf_op jit(solution)/shard_map/pallas_call | solution.py:258
  29.6 1.0 %collective-permute-done.9.refs_1_ = s16[144,1024]{1,0:T(8,128)(2,1)S(1)} collective-permute-done((s16[144,1024]{1,0:T(8,128)(2,1)S(1)}, s16[144,1024]{1,0:T(8,128)(2,1)S(1)}, u32[]{:S(2)}, u32[]{:S(2)}) %collective-permute-start.9) | collective-permute-done | bytes 294944 | tf_op jit(solution)/shard_map/ppermute | solution.py:374
  30.6 0.4 %shard_map.76 = (s16[144,256]{1,0:T(8,128)(2,1)S(1)}, s16[144,256]{1,0:T(8,128)(2,1)S(1)}, s16[144,256]{1,0:T(8,128)(2,1)S(1)}, s16[144,256]{1,0:T(8,128)(2,1)S(1)}) custom-call(s16[144,1024]{1,0:T(8,128)(2,1)S(1)} %shard_map.74.refs_0_, s16[144,1024]{1,0:T(8,128)(2,1)S(1)} %collective-permute-done.9.refs_1_), custom_call_target="tpu_custom_call" | custom-call | tf_op jit(solution)/shard_map/pallas_call | solution.py:298
  31.0 0.1 collective-permute-start.10
  31.1 3.3 %collective-permute-start.11 = (s16[144,256]{1,0:T(8,128)(2,1)S(1)}, s16[144,256]{1,0:T(8,128)(2,1)S(1)}, u32[]{:S(2)}, u32[]{:S(2)}) collective-permute-start(s16[144,256]{1,0:T(8,128)(2,1)S(1)} %get-tuple-element.35), channel_id=1, source_target_pairs={{0,10},{1,13},{2,8},{3,15},{4,14},{5,9},{6,12},{7,11},{8,2},{9,5},... | collective-permute-start | bytes 221192 | tf_op jit(solution)/shard_map/ppermute | solution.py:374
  34.5 1.0 %collective-permute-start.12 = (s16[144,256]{1,0:T(8,128)(2,1)S(1)}, s16[144,256]{1,0:T(8,128)(2,1)S(1)}, u32[]{:S(2)}, u32[]{:S(2)}) collective-permute-start(s16[144,256]{1,0:T(8,128)(2,1)S(1)} %get-tuple-element.36), channel_id=1, source_target_pairs={{0,8},{1,5},{2,10},{3,7},{4,12},{5,1},{6,14},{7,3},{8,0},{9,13},{1... | collective-permute-start | bytes 221192 | tf_op jit(solution)/shard_map/ppermute | solution.py:374
  35.5 0.0 collective-permute-done.10.refs_1_
  35.5 2.0 %collective-permute-done.11.refs_2_ = s16[144,256]{1,0:T(8,128)(2,1)S(1)} collective-permute-done((s16[144,256]{1,0:T(8,128)(2,1)S(1)}, s16[144,256]{1,0:T(8,128)(2,1)S(1)}, u32[]{:S(2)}, u32[]{:S(2)}) %collective-permute-start.11) | collective-permute-done | bytes 73760 | tf_op jit(solution)/shard_map/ppermute | solution.py:374
  37.4 2.4 %collective-permute-done.12.refs_3_ = s16[144,256]{1,0:T(8,128)(2,1)S(1)} collective-permute-done((s16[144,256]{1,0:T(8,128)(2,1)S(1)}, s16[144,256]{1,0:T(8,128)(2,1)S(1)}, u32[]{:S(2)}, u32[]{:S(2)}) %collective-permute-start.12) | collective-permute-done | bytes 73760 | tf_op jit(solution)/shard_map/ppermute | solution.py:374
  39.8 0.2 shard_map.77
  40.0 0.1 collective-permute-start.13
  40.1 1.2 %collective-permute-done.13.theirs = bf16[4,4096]{1,0:T(4,128)(2,1)S(1)} collective-permute-done((bf16[4,4096]{1,0:T(4,128)(2,1)S(1)}, bf16[4,4096]{1,0:T(4,128)(2,1)S(1)}, u32[]{:S(2)}, u32[]{:S(2)}) %collective-permute-start.13) | collective-permute-done | bytes 32800 | tf_op jit(solution)/shard_map/ppermute | solution.py:365
  41.3 0.6 %shard_map.78 = bf16[4,8192]{1,0:T(4,128)(2,1)} custom-call(bf16[4,4096]{1,0:T(4,128)(2,1)S(1)} %get-tuple-element.37.mine, bf16[4,4096]{1,0:T(4,128)(2,1)S(1)} %collective-permute-done.13.theirs), custom_call_target="tpu_custom_call" | custom-call | tf_op jit(solution)/shard_map/pallas_call | solution.py:344
  (3 shorter events, 0.0 us)
Async XLA Ops:
  0.0 1.9 %collective-permute-start = (s32[1]{0:T(128)}, s32[1]{0:T(128)}, u32[]{:S(2)}, u32[]{:S(2)}) collective-permute-start(s32[1]{0:T(128)} %param.12), channel_id=1, source_target_pairs={{0,1},{1,0},{2,3},{3,2},{4,5},{5,4},{6,7},{7,6},{8,9},{9,8},{10,11... | collective-permute-start | bytes 20 | tf_op jit(solution)/shard_map/ppermute | solution.py:365
  0.5 1.5 %collective-permute-start.1 = (bf16[4,8192]{1,0:T(4,128)(2,1)}, bf16[4,8192]{1,0:T(4,128)(2,1)S(1)}, u32[]{:S(2)}, u32[]{:S(2)}) collective-permute-start(bf16[4,8192]{1,0:T(4,128)(2,1)} %param.7), channel_id=1, source_target_pairs={{0,1},{1,0},{2,3},{3,2},{4,5},{5,4},{6,7},{7,6},{8,9},{9,8},{10,11... | collective-permute-start | bytes 196616 | tf_op jit(solution)/shard_map/ppermute | solution.py:365
  2.7 16.5 %collective-permute-start.7 = (bf16[1536,512]{1,0:T(8,128)(2,1)}, bf16[1536,512]{1,0:T(8,128)(2,1)S(1)}, u32[]{:S(2)}, u32[]{:S(2)}) collective-permute-start(bf16[1536,512]{1,0:T(8,128)(2,1)} %param.8), channel_id=1, source_target_pairs={{0,1},{1,0},{2,3},{3,2},{4,5},{5,4},{6,7},{7,6},{8,9},{9,8},{10,11... | collective-permute-start | bytes 4718600 | tf_op jit(solution)/shard_map/ppermute | solution.py:365
  3.2 16.0 %collective-permute-start.8 = (bf16[1536,512]{1,0:T(8,128)(2,1)}, bf16[1536,512]{1,0:T(8,128)(2,1)S(1)}, u32[]{:S(2)}, u32[]{:S(2)}) collective-permute-start(bf16[1536,512]{1,0:T(8,128)(2,1)} %param.9), channel_id=1, source_target_pairs={{0,1},{1,0},{2,3},{3,2},{4,5},{5,4},{6,7},{7,6},{8,9},{9,8},{10,11... | collective-permute-start | bytes 4718600 | tf_op jit(solution)/shard_map/ppermute | solution.py:365
  3.3 6.3 %collective-permute-start.2 = (bf16[8,4224]{1,0:T(8,128)(2,1)S(1)}, bf16[8,4224]{1,0:T(8,128)(2,1)S(1)}, u32[]{:S(2)}, u32[]{:S(2)}) collective-permute-start(bf16[8,4224]{1,0:T(8,128)(2,1)S(1)} %shard_map.73), channel_id=1, source_target_pairs={{0,8},{1,5},{2,10},{3,7},{4,12},{5,1},{6,14},{7,3},{8,0},{9,13},{1... | collective-permute-start | bytes 202760 | tf_op jit(solution)/shard_map/ppermute | solution.py:374
  9.6 6.5 %copy-start = (bf16[4,512]{1,0:T(4,128)(2,1)S(1)}, bf16[4,512]{1,0:T(4,128)(2,1)}, u32[]{:S(2)}) copy-start(bf16[4,512]{1,0:T(4,128)(2,1)} %param.11) | copy-start | bytes 12292
  9.6 6.5 %copy-start.1 = (bf16[4,512]{1,0:T(4,128)(2,1)S(1)}, bf16[4,512]{1,0:T(4,128)(2,1)}, u32[]{:S(2)}) copy-start(bf16[4,512]{1,0:T(4,128)(2,1)} %param.10) | copy-start | bytes 12292
  9.6 6.5 %collective-permute-start.5 = (bf16[16,4224]{1,0:T(8,128)(2,1)S(1)}, bf16[16,4224]{1,0:T(8,128)(2,1)S(1)}, u32[]{:S(2)}, u32[]{:S(2)}) collective-permute-start(bf16[16,4224]{1,0:T(8,128)(2,1)S(1)} %constant_dynamic-update-slice_fusion.refs_1_), channel_id=1, source_target_pairs={{0,6},{1,11},{2,4},{3,9},{4,2},{5,15},{6,0},{7,13},{8,14},{9,3},{1... | collective-permute-start | bytes 405512 | tf_op jit(solution)/shard_map/ppermute | solution.py:374
  12.5 6.7 %collective-permute-start.4 = (bf16[16,4224]{1,0:T(8,128)(2,1)S(1)}, bf16[16,4224]{1,0:T(8,128)(2,1)S(1)}, u32[]{:S(2)}, u32[]{:S(2)}) collective-permute-start(bf16[16,4224]{1,0:T(8,128)(2,1)S(1)} %constant_dynamic-update-slice_fusion.refs_1_), channel_id=1, source_target_pairs={{0,4},{1,3},{2,6},{3,1},{4,0},{5,7},{6,2},{7,5},{8,12},{9,11},{10,... | collective-permute-start | bytes 405512 | tf_op jit(solution)/shard_map/ppermute | solution.py:374
  13.0 6.2 %collective-permute-start.3 = (bf16[16,4224]{1,0:T(8,128)(2,1)S(1)}, bf16[16,4224]{1,0:T(8,128)(2,1)S(1)}, u32[]{:S(2)}, u32[]{:S(2)}) collective-permute-start(bf16[16,4224]{1,0:T(8,128)(2,1)S(1)} %constant_dynamic-update-slice_fusion.refs_1_), channel_id=1, source_target_pairs={{0,2},{1,9},{2,0},{3,11},{4,6},{5,13},{6,4},{7,15},{8,10},{9,1},{1... | collective-permute-start | bytes 405512 | tf_op jit(solution)/shard_map/ppermute | solution.py:374
  16.1 3.1 %collective-permute-start.6 = (bf16[8,512]{1,0:T(8,128)(2,1)S(1)}, bf16[8,512]{1,0:T(8,128)(2,1)S(1)}, u32[]{:S(2)}, u32[]{:S(2)}) collective-permute-start(bf16[8,512]{1,0:T(8,128)(2,1)S(1)} %pad_maximum_fusion.refs_5_), channel_id=1, source_target_pairs={{0,1},{1,0},{2,3},{3,2},{4,5},{5,4},{6,7},{7,6},{8,9},{9,8},{10,11... | collective-permute-start | bytes 24584 | tf_op jit(solution)/shard_map/ppermute | solution.py:365
  23.8 6.8 %collective-permute-start.9 = (s16[144,1024]{1,0:T(8,128)(2,1)S(1)}, s16[144,1024]{1,0:T(8,128)(2,1)S(1)}, u32[]{:S(2)}, u32[]{:S(2)}) collective-permute-start(s16[144,1024]{1,0:T(8,128)(2,1)S(1)} %shard_map.75), channel_id=1, source_target_pairs={{0,4},{1,3},{2,6},{3,1},{4,0},{5,7},{6,2},{7,5},{8,12},{9,11},{10,... | collective-permute-start | bytes 884744 | tf_op jit(solution)/shard_map/ppermute | solution.py:374
  31.0 4.5 %collective-permute-start.10 = (s16[144,256]{1,0:T(8,128)(2,1)S(1)}, s16[144,256]{1,0:T(8,128)(2,1)S(1)}, u32[]{:S(2)}, u32[]{:S(2)}) collective-permute-start(s16[144,256]{1,0:T(8,128)(2,1)S(1)} %get-tuple-element.34), channel_id=1, source_target_pairs={{0,2},{1,9},{2,0},{3,11},{4,6},{5,13},{6,4},{7,15},{8,10},{9,1},{1... | collective-permute-start | bytes 221192 | tf_op jit(solution)/shard_map/ppermute | solution.py:374
  31.1 6.3 %collective-permute-start.11 = (s16[144,256]{1,0:T(8,128)(2,1)S(1)}, s16[144,256]{1,0:T(8,128)(2,1)S(1)}, u32[]{:S(2)}, u32[]{:S(2)}) collective-permute-start(s16[144,256]{1,0:T(8,128)(2,1)S(1)} %get-tuple-element.35), channel_id=1, source_target_pairs={{0,10},{1,13},{2,8},{3,15},{4,14},{5,9},{6,12},{7,11},{8,2},{9,5},... | collective-permute-start | bytes 221192 | tf_op jit(solution)/shard_map/ppermute | solution.py:374
  34.5 5.3 %collective-permute-start.12 = (s16[144,256]{1,0:T(8,128)(2,1)S(1)}, s16[144,256]{1,0:T(8,128)(2,1)S(1)}, u32[]{:S(2)}, u32[]{:S(2)}) collective-permute-start(s16[144,256]{1,0:T(8,128)(2,1)S(1)} %get-tuple-element.36), channel_id=1, source_target_pairs={{0,8},{1,5},{2,10},{3,7},{4,12},{5,1},{6,14},{7,3},{8,0},{9,13},{1... | collective-permute-start | bytes 221192 | tf_op jit(solution)/shard_map/ppermute | solution.py:374
  40.0 1.3 %collective-permute-start.13 = (bf16[4,4096]{1,0:T(4,128)(2,1)S(1)}, bf16[4,4096]{1,0:T(4,128)(2,1)S(1)}, u32[]{:S(2)}, u32[]{:S(2)}) collective-permute-start(bf16[4,4096]{1,0:T(4,128)(2,1)S(1)} %get-tuple-element.38), channel_id=1, source_target_pairs={{0,1},{1,0},{2,3},{3,2},{4,5},{5,4},{6,7},{7,6},{8,9},{9,8},{10,11... | collective-permute-start | bytes 98312 | tf_op jit(solution)/shard_map/ppermute | solution.py:365
